TPU v7x, 1024 devices: a whole 8x8x8 slice. The times are simulated.
1024 devices in a mesh: seq: 128 (over z, y, core), head: 8 (over x).
Axes of the slice: x: 8, y: 8, z: 8, core: 2. Of those that a mesh axis runs over, the one named last changes fastest.
Arguments:
- queries: bfloat16 [16384, 4096], P('seq', 'head'), may hold values from -6 to 6
- keys: bfloat16 [16384, 4096], P('seq', 'head'), may hold values from -0.059814453 to 0.059814453
- values: bfloat16 [16384, 4096], P('seq', 'head'), may hold values from -6 to 6
- d_out: bfloat16 [16384, 4096], P('seq', 'head'), may hold values from -6 to 6
- segment_ids: int32 [16384], P('seq'), may hold values from 0 to 7, never falling along the last dimension, each value on 1 to 4096 neighbouring positions
- decay_exps: int32 [32], P('head'), may hold values from 0 to 12
- gain: float32 [4096], P('head'), may hold values from 0.25 to 1.75
Outputs:
- normed: float32 [16384, 4096], P('seq', 'head')
- d_queries: float32 [16384, 4096], P('seq', 'head')
- d_keys: float32 [16384, 4096], P('seq', 'head')
- d_values: float32 [16384, 4096], P('seq', 'head')
Inputs may be any that keep to these rules, and one draw needn't show every extreme that they name: `segment_ids`: segment ids never fall along the tokens; each document has 1 to 4096 tokens, one exactly that many.
All inputs are finite; a program needn't handle non-finite values.
Results may differ from a plain program's by a relative error of at most 0.0012.
Values sent between devices are 32-bit elements; how exact they have to be, the bound alone decides.
A program may use at most 128 MiB of HBM per device.

v0:
```python
import jax
import jax.numpy as jnp
from jax import lax
from jax.sharding import PartitionSpec as P

DH = 128


EPSILON = 1e-06
HIGH = lax.Precision.HIGHEST


def entering(array, axis, combine, identity, reverse):
    size, position = (lax.axis_size(axis), lax.axis_index(axis))
    everything = jax.tree.map(lambda part: lax.all_gather(part, axis), array)
    start = jax.tree.map(
        lambda part, zero: jnp.broadcast_to(jnp.asarray(zero, part.dtype), part.shape),
        array,
        identity,
    )

    def hop(k, before):
        at = size - 1 - k if reverse else k
        reached = at > position if reverse else at < position
        new = combine(before, jax.tree.map(lambda part: part[at], everything))
        return jax.tree.map(lambda a, b: jnp.where(reached, a, b), new, before)

    return lax.fori_loop(0, size, hop, start)


def forward_combine(earlier, later):
    e_decay, e_state, e_first, e_last = earlier
    l_decay, l_state, l_first, l_last = later
    later_empty = l_last < 0
    keep_on = (l_first == l_last) & (e_last == l_first)
    joined = jnp.where(keep_on, l_decay[:, None, None] * e_state + l_state, l_state)
    state = jnp.where(later_empty, e_state, joined)
    first_seg = jnp.where(e_first < 0, l_first, e_first)
    last_seg = jnp.where(later_empty, e_last, l_last)
    return (e_decay * l_decay, state, first_seg, last_seg)


def backward_combine(earlier, later):
    e_decay, e_state, e_first, e_last = earlier
    l_decay, l_state, l_first, l_last = later
    later_empty = l_last < 0
    keep_on = (l_first == l_last) & (l_last == e_first)
    joined = jnp.where(keep_on, l_state + l_decay[:, None, None] * e_state, l_state)
    state = jnp.where(later_empty, e_state, joined)
    first_seg = jnp.where(later_empty, e_first, l_first)
    last_seg = jnp.where(e_last < 0, l_last, e_last)
    return (e_decay * l_decay, state, first_seg, last_seg)


def body(queries, keys, values, d_out, segment_ids, decay_exps, gain):
    tok_rows = queries.shape[0]
    head_count = queries.shape[1] // DH
    seq_count = lax.axis_size("seq")
    total_tokens = tok_rows * seq_count
    decay_rate = jnp.exp2(decay_exps.astype(jnp.float32)) / total_tokens

    def heads_first(array):
        return array.reshape(tok_rows, head_count, DH).transpose(1, 0, 2)

    queries_h = heads_first(queries)
    keys_h = heads_first(keys)
    values_h = heads_first(values)
    grads_h = heads_first(d_out)
    seg_float = segment_ids.astype(jnp.float32)
    place = jnp.arange(tok_rows, dtype=jnp.float32)
    distance = place[:, None] - place[None, :]
    causal_mask = (distance >= 0) & (segment_ids[:, None] == segment_ids[None, :])
    decay = jnp.where(
        causal_mask[None],
        jnp.exp(-decay_rate[:, None, None] * jnp.maximum(distance, 0.0)[None]),
        0.0,
    )
    span_decay = jnp.exp(-decay_rate * tok_rows)
    endw = (
        jnp.exp(-decay_rate[:, None] * (tok_rows - 1.0 - place)[None, :])
        * (seg_float == seg_float[-1])[None, :]
    )
    startw = jnp.exp(-decay_rate[:, None] * place[None, :]) * (seg_float == seg_float[0])[None, :]
    zero_state = jnp.zeros((head_count, DH, DH), jnp.float32)
    identity = (
        jnp.ones((head_count,), jnp.float32),
        zero_state,
        jnp.float32(-1.0),
        jnp.float32(-1.0),
    )

    def weighted_state(weights, left, right):
        scaled = weights[:, :, None] * left.astype(jnp.float32)
        return jnp.einsum("htd,hte->hde", scaled, right.astype(jnp.float32), precision=HIGH)

    element = (span_decay, weighted_state(endw, keys_h, values_h), seg_float[0], seg_float[-1])
    prefix = entering(element, "seq", forward_combine, identity, False)
    incoming = prefix[1]
    inflow = (
        jnp.exp(-decay_rate[:, None] * (place + 1.0)[None, :]) * (seg_float == prefix[3])[None, :]
    )
    scores = (
        jnp.einsum("htd,hsd->hts", queries_h, keys_h, preferred_element_type=jnp.float32) * decay
    ).astype(jnp.bfloat16)
    grad_scores = (
        jnp.einsum("hte,hse->hts", grads_h, values_h, preferred_element_type=jnp.float32) * decay
    ).astype(jnp.bfloat16)
    output = jnp.einsum("hts,hse->hte", scores, values_h, preferred_element_type=jnp.float32)
    output = output + inflow[:, :, None] * jnp.einsum(
        "htd,hde->hte", queries_h.astype(jnp.float32), incoming, precision=HIGH
    )
    grad_q = jnp.einsum("hts,hsd->htd", grad_scores, keys_h, preferred_element_type=jnp.float32)
    grad_q = grad_q + inflow[:, :, None] * jnp.einsum(
        "hte,hde->htd", grads_h.astype(jnp.float32), incoming, precision=HIGH
    )
    output, grad_q, scores, grad_scores = (output, grad_q, scores, grad_scores)
    element = (span_decay, weighted_state(startw, queries_h, grads_h), seg_float[0], seg_float[-1])
    suffix = entering(element, "seq", backward_combine, identity, True)
    incoming = suffix[1]
    outw = (
        jnp.exp(-decay_rate[:, None] * (tok_rows - place)[None, :])
        * (seg_float == suffix[2])[None, :]
    )
    grad_k = jnp.einsum("hts,htd->hsd", grad_scores, queries_h, preferred_element_type=jnp.float32)
    grad_k = grad_k + outw[:, :, None] * jnp.einsum(
        "hse,hde->hsd", values_h.astype(jnp.float32), incoming, precision=HIGH
    )
    grad_v = jnp.einsum("hts,hte->hse", scores, grads_h, preferred_element_type=jnp.float32)
    grad_v = grad_v + outw[:, :, None] * jnp.einsum(
        "hsd,hde->hse", keys_h.astype(jnp.float32), incoming, precision=HIGH
    )
    grad_k, grad_v = (grad_k, grad_v)
    square_sum = lax.psum(jnp.sum(output * output, axis=(0, 2)), "head")
    width_all = head_count * lax.axis_size("head") * DH
    inverse = lax.rsqrt(square_sum / width_all + EPSILON)
    normed = output * inverse[None, :, None] * gain.reshape(head_count, 1, DH)
    width = head_count * DH

    def tokens_first(array):
        return array.transpose(1, 0, 2).reshape(tok_rows, width)

    return (tokens_first(normed), tokens_first(grad_q), tokens_first(grad_k), tokens_first(grad_v))


def solution(mesh):
    in_specs = (
        P("seq", "head"),
        P("seq", "head"),
        P("seq", "head"),
        P("seq", "head"),
        P("seq"),
        P("head"),
        P("head"),
    )
    out_specs = (P("seq", "head"), P("seq", "head"), P("seq", "head"), P("seq", "head"))
    return jax.shard_map(body, mesh=mesh, in_specs=in_specs, out_specs=out_specs, check_vma=False)
```

profile of v0, /device:TPU:1, one launch (start us, length us, event | category | flops | bytes accessed | tf_op | source)
XLA Modules:
  0.0 1792.2 jit_solution(3230845530053745832)
XLA Ops:
  7.9 1.3 dynamic-slice
  9.8 1.2 fusion.33
  11.0 1.3 compare_convert_fusion.1
  15.2 1.1 fusion.13
  17.2 264.2 %all-reduce.3 = (f32[128]{0:T(128)S(1)}, f32[128]{0:T(128)S(1)}, f32[512]{0:T(512)S(1)}) all-reduce(f32[128]{0:T(128)S(1)} %get-tuple-element.453, f32[128]{0:T(128)S(1)} %slice_dynamic-update-slice_fusion, f32[512]{0:T(512)S(1)} %get-tuple-element.456), channel_id=1, replica_groups=mesh['seq'=128,'head'=8] {'seq'}, use_global_device_ids=true, to_apply=%add | all-reduce | flops 768 | bytes 6144
  281.6 667.7 %while.35 = (s32[]{:T(128)}, f32[4,128,128]{2,1,0:T(8,128)S(1)}, f32[]{:T(128)}, s32[]{:T(128)}, f32[128]{0:T(128)S(1)}, /*index=5*/f32[128]{0:T(128)S(1)}, f32[...) while((s32[]{:T(128)}, f32[4,128,128]{2,1,0:T(8,128)S(1)}, ...), condition=%wide.region_5.6_spmd.clone, body=%wide.region_4.5_spmd.clone.sunk | while | flops 393230 | bytes 786761 | solution.py:28
  285.0 1.1 select_select_fusion.5
  290.3 1.1 select_select_fusion.5
  305.9 1.1 select_select_fusion.5
  311.1 1.1 select_select_fusion.5
  316.3 1.1 select_select_fusion.5
  326.8 1.1 select_select_fusion.5
  332.0 1.1 select_select_fusion.5
  337.2 1.1 select_select_fusion.5
  352.9 1.1 select_select_fusion.5
  358.1 1.1 select_select_fusion.5
  363.3 1.1 select_select_fusion.5
  378.9 1.1 select_select_fusion.5
  384.2 1.1 select_select_fusion.5
  389.4 1.1 select_select_fusion.5
  405.0 1.1 select_select_fusion.5
  410.2 1.1 select_select_fusion.5
  415.5 1.1 select_select_fusion.5
  425.9 1.1 select_select_fusion.5
  431.1 1.1 select_select_fusion.5
  436.3 1.1 select_select_fusion.5
  452.0 1.1 select_select_fusion.5
  457.2 1.1 select_select_fusion.5
  462.4 1.1 select_select_fusion.5
  478.1 1.1 select_select_fusion.5
  483.3 1.1 select_select_fusion.5
  488.5 1.1 select_select_fusion.5
  504.1 1.1 select_select_fusion.5
  509.3 1.1 select_select_fusion.5
  514.6 1.1 select_select_fusion.5
  525.0 1.1 select_select_fusion.5
  530.2 1.1 select_select_fusion.5
  535.4 1.1 select_select_fusion.5
  551.1 1.1 select_select_fusion.5
  556.3 1.1 select_select_fusion.5
  561.5 1.1 select_select_fusion.5
  577.2 1.1 select_select_fusion.5
  582.4 1.1 select_select_fusion.5
  587.6 1.1 select_select_fusion.5
  603.2 1.1 select_select_fusion.5
  608.5 1.1 select_select_fusion.5
  613.7 1.1 select_select_fusion.5
  624.1 1.1 select_select_fusion.5
  629.3 1.1 select_select_fusion.5
  634.5 1.1 select_select_fusion.5
  650.2 1.1 select_select_fusion.5
  655.4 1.1 select_select_fusion.5
  660.6 1.1 select_select_fusion.5
  676.3 1.1 select_select_fusion.5
  681.5 1.1 select_select_fusion.5
  686.7 1.1 select_select_fusion.5
  949.3 1.2 compare_convert_fusion
  950.5 2.1 fusion.16
  953.5 1.1 fusion.6
  955.1 1.1 convolution_bitcast_fusion.5
  956.5 140.8 %all-gather.6.cloned.1.call-done = f32[512,128,128]{2,1,0:T(8,128)} async-done(((f32[4,128,128]{2,1,0:T(8,128)}), f32[512,128,128]{2,1,0:T(8,128)}) %all-gather.6.cloned.1.call-update) | async-done | bytes 33554448 | tf_op jit(solution)/shard_map/all_gather | solution.py:15
  1097.3 667.1 %while.34 = (s32[]{:T(128)}, f32[4,128,128]{2,1,0:T(8,128)S(1)}, f32[]{:T(128)}, s32[]{:T(128)}, f32[128]{0:T(128)S(1)}, /*index=5*/f32[128]{0:T(128)S(1)}, f32[...) while((s32[]{:T(128)}, f32[4,128,128]{2,1,0:T(8,128)S(1)}, ...), condition=%wide.region_1.2_spmd.clone, body=%wide.region_0.1_spmd.clone.sunk | while | flops 393226 | bytes 786699 | solution.py:28
  1765.2 1.3 fusion.1
  1770.3 13.3 psum.7
  (1014 shorter events, 527.5 us)
Async XLA Ops:
  7.2 943.4 %copy-start = (bf16[128,512]{1,0:T(8,128)(2,1)S(1)}, bf16[128,512]{1,0:T(8,128)(2,1)}, u32[]{:S(2)}) copy-start(bf16[128,512]{1,0:T(8,128)(2,1)} %param.13) | copy-start | bytes 393220
  7.2 274.4 %all-gather.8.cloned.1.call-start = ((), (), s32[]{:S(2)}) async-start(), calls=%async_computation.1 | async-start | bytes 33816576 | tf_op jit(solution)/shard_map/all_gather | solution.py:15
  16.4 1080.9 %all-gather.6.cloned.1.call-start = ((), (), s32[]{:S(2)}) async-start(), calls=%async_computation | async-start | bytes 33816576 | tf_op jit(solution)/shard_map/all_gather | solution.py:15
Sparse Core Ops, SparseCore 0:
  16.5 162.3 all-gather.7
  952.8 144.4 all-gather.5
where the time goes:
time: 1810 us; the launch traced here: 1790 us
  loops' own time  766 us (42%)
  local copies, waits for them, and re-layouts  303 us (17%)
  other arithmetic  281 us (16%)
  blocking collectives  278 us (15%)
  waiting for transfers between devices  141 us (8%)
    another operation x2, loops' own time, entering(): return lax.fori_loop(0, size, hop, start)  766 us
    dynamic_slice x512, local copies, waits for them, and re-layouts, hop(): new = combine(before, jax.tree.map(lambda part: part[at], everything))  292 us
    select_n x256, other arithmetic, hop(): return jax.tree.map(lambda a, b: jnp.where(reached, a, b), new, before)  274 us
    unnamed x1, blocking collectives  264 us
    all_gather x2, waiting for transfers between devices, entering(): everything = jax.tree.map(lambda part: lax.all_gather(part, axis), array)  141 us
  transfers between devices with their start and end apart: 2, of which 1 were waited for; matrix products, arithmetic and copies ran while one was open for 0% of the time, Pallas kernels for 0%

commit v1 on v0

v1 whole, which is shorter than its diff:
```python
import functools

import jax
import jax.numpy as jnp
from jax import lax
from jax.experimental import pallas as pl
from jax.experimental.pallas import tpu as pltpu
from jax.sharding import PartitionSpec as P

DH = 128
BLK = 128
NH = 4
OWN = 2
ROW = 8
EPSILON = 1e-06
MESH = pl.DeviceIdType.MESH
F32 = jnp.float32
BF16 = jnp.bfloat16

NN = (((1,), (0,)), ((), ()))
NT = (((1,), (1,)), ((), ()))
TN = (((0,), (0,)), ((), ()))


def dot(a, b, dims):
    return lax.dot_general(a, b, dims, preferred_element_type=F32)


def split(a):
    high = a.astype(BF16)
    return high, (a - high.astype(F32)).astype(BF16)


def kernel(
    zs, xs, exps, seg, q, k, v, g, gain,
    normed, dq, dk, dv,
    local, part, mymeta, pmeta, chip, cmeta, rmeta, there, zsend, zrecv, slices, raw, give, state, out, xsend, xrecv,
    d_send, d_recv, m_send, m_recv, t_send, t_recv, z_send, z_recv, b_send, b_recv, e_send, e_recv, x_send, x_recv,
):
    s, x = lax.axis_index("seq"), lax.axis_index("head")
    c, y, z = s % 2, (s // 2) % ROW, s // (2 * ROW)
    width = BLK // ROW
    total_tokens = BLK * 2 * ROW * zs

    def at(zz, yy, cc):
        return ((zz * ROW + yy) * 2 + cc, x)

    partner = at(z, y, 1 - c)
    in_row = [(y + n) % ROW for n in range(1, ROW)]

    def hop(way, n):
        return at((z + (n if way == 0 else zs - n)) % zs, y, c)

    def copy(src, dst, send, recv, device):
        return pltpu.make_async_remote_copy(
            src_ref=src, dst_ref=dst, send_sem=send, recv_sem=recv, device_id=device, device_id_type=MESH
        )

    barrier = pltpu.get_barrier_semaphore()
    others = [partner] + [at(z, j, c) for j in in_row] + [hop(w, n) for w in (0, 1) for n in (1, 2)]
    others += [(s, (x + n) % xs) for n in range(1, xs)]
    for device in others:
        pl.semaphore_signal(barrier, inc=1, device_id=device, device_id_type=MESH)

    place = lax.broadcasted_iota(jnp.int32, (BLK, DH), 0).astype(F32)
    seg_row = seg[...].astype(F32)
    seg_rows = jnp.broadcast_to(seg_row, (BLK, BLK))
    seg_cols = seg_rows.T
    first = jnp.broadcast_to(seg_cols[0:1, :], (8, DH))
    last = jnp.broadcast_to(seg_cols[BLK - 1 : BLK, :], (8, DH))
    row_id = lax.broadcasted_iota(jnp.int32, (8, DH), 0)
    mymeta[...] = jnp.where(row_id == 0, first, last)

    def rate_of(h):
        whole = jnp.left_shift(jnp.ones((1, DH), jnp.int32), jnp.full((1, DH), exps[h], jnp.int32))
        return whole.astype(F32) / total_tokens

    rates = [rate_of(h) for h in range(NH)]
    own_rates = [rate_of(OWN * c + i) for i in range(OWN)]
    cols = [slice(h * DH, (h + 1) * DH) for h in range(NH)]

    def weighted(weight, left, right):
        high, low = split(weight * left.astype(F32))
        return dot(high, right, TN) + dot(low, right, TN)

    ends = (seg_cols == last[0:1, :]).astype(F32)
    starts = (seg_cols == first[0:1, :]).astype(F32)
    for h in range(NH):
        weight = jnp.exp(-rates[h] * (BLK - 1.0 - place)) * ends
        local[0, h] = weighted(weight, k[:, cols[h]], v[:, cols[h]])

    pl.semaphore_wait(barrier, len(others))

    meta_copy = copy(mymeta, pmeta, m_send.at[0], m_recv.at[0], partner)
    meta_copy.start()
    sends = [meta_copy]

    def to_partner(way):
        found = []
        for i in range(OWN):
            found.append(
                copy(local.at[way, OWN * (1 - c) + i], part.at[way, i], d_send.at[way, i], d_recv.at[way, i], partner)
            )
            found[-1].start()
        sends.extend(found)
        return found

    first_copies = [to_partner(0)]
    for h in range(NH):
        weight = jnp.exp(-rates[h] * place) * starts
        local[1, h] = weighted(weight, q[:, cols[h]], g[:, cols[h]])
    first_copies.append(to_partner(1))

    meta_copy.wait_recv()
    firsts = [jnp.where(c == 0, mymeta[0:1, :], pmeta[0:1, :]), jnp.where(c == 0, pmeta[0:1, :], mymeta[0:1, :])]
    lasts = [jnp.where(c == 0, mymeta[1:2, :], pmeta[1:2, :]), jnp.where(c == 0, pmeta[1:2, :], mymeta[1:2, :])]
    chip_meta = jnp.where(row_id == 0, jnp.broadcast_to(firsts[0], (8, DH)), jnp.broadcast_to(lasts[1], (8, DH)))
    cmeta[...] = chip_meta
    rmeta[y] = chip_meta
    row_meta = []
    for n, j in enumerate(in_row):
        row_meta.append(copy(cmeta, rmeta.at[y], m_send.at[1 + n], m_recv.at[1 + y], at(z, j, c)))
        row_meta[-1].start()
    sends.extend(row_meta)
    same_chip = [(lasts[0] == lasts[1]).astype(F32), (firsts[0] == firsts[1]).astype(F32)]

    def to_row(way):
        for i in range(OWN):
            first_copies[way][i].wait_recv()
            carried = jnp.exp(-own_rates[i] * BLK) * same_chip[way]
            mine = jnp.where(c == 1 - way, 1.0, carried)
            theirs = jnp.where(c == 1 - way, carried, 1.0)
            whole = mine * local[way, OWN * c + i] + theirs * part[way, i]
            chip[way, i] = whole
            there[way, i, y] = chip[way, i, pl.ds(pl.multiple_of(y * width, width), width), :]
            for n, j in enumerate(in_row):
                sends.append(
                    copy(
                        chip.at[way, i, pl.ds(pl.multiple_of(j * width, width), width)],
                        there.at[way, i, y],
                        t_send.at[way, i, n],
                        t_recv.at[way, i, y],
                        at(z, j, c),
                    )
                )
                sends[-1].start()

    to_row(0)
    to_row(1)

    distance = place - lax.broadcasted_iota(jnp.int32, (BLK, DH), 1).astype(F32)
    causal = (distance >= 0) & (seg_cols == seg_rows)
    reach = jnp.maximum(distance, 0.0)

    def within(h):
        decay = jnp.where(causal, jnp.exp(-rates[h] * reach), 0.0)
        qh, kh, vh, gh = q[:, cols[h]], k[:, cols[h]], v[:, cols[h]], g[:, cols[h]]
        scores = (dot(qh, kh, NT) * decay).astype(BF16)
        grad_scores = (dot(gh, vh, NT) * decay).astype(BF16)
        out[:, cols[h]] = dot(scores, vh, NN)
        dq[:, cols[h]] = dot(grad_scores, kh, NN)
        dk[:, cols[h]] = dot(grad_scores, qh, TN)
        dv[:, cols[h]] = dot(scores, gh, TN)

    within(0)
    within(1)

    for j in in_row:
        copy(cmeta, rmeta.at[j], m_send.at[0], m_recv.at[1 + j], partner).wait_recv()

    def end_of(way, j):
        return rmeta[j, 1:2, :] if way == 0 else rmeta[j, 0:1, :]

    orders = [list(range(ROW)), list(range(ROW))[::-1]]

    def to_rows(way):
        order = orders[way]
        zsend[way, 0:8] = jnp.broadcast_to(end_of(way, order[-1]), (8, DH))
        for i in range(OWN):
            for j in in_row:
                copy(
                    there.at[way, i, y], there.at[way, i, j], t_send.at[way, i, 0], t_recv.at[way, i, j], partner
                ).wait_recv()
            span = jnp.exp(-own_rates[i] * (2 * BLK))
            sofar = there[way, i, order[0]]
            for n in range(1, ROW):
                slices[way, i, order[n]] = sofar
                keep = span * (end_of(way, order[n]) == end_of(way, order[n - 1])).astype(F32)
                sofar = there[way, i, order[n]] + keep * sofar
            low, high = (0, 8 + width) if i == 0 else (8 + width, 8 + 2 * width)
            zsend[way, 8 + i * width : 8 + (i + 1) * width] = sofar
            for n in (1, 2):
                sends.append(
                    copy(
                        zsend.at[way, low:high],
                        zrecv.at[way, n - 1, low:high],
                        z_send.at[way, n - 1, i],
                        z_recv.at[way, n - 1, i],
                        hop(way, n),
                    )
                )
                sends[-1].start()

    to_rows(0)
    to_rows(1)
    within(2)
    within(3)

    edge = [None, None]

    def to_chips(way):
        order = orders[way]
        left = z if way == 0 else zs - 1 - z
        for i in range(OWN):
            low, high = (0, 8 + width) if i == 0 else (8 + width, 8 + 2 * width)
            for n in (1, 2):
                copy(
                    zsend.at[way, low:high],
                    zrecv.at[way, n - 1, low:high],
                    z_send.at[way, n - 1, i],
                    z_recv.at[way, n - 1, i],
                    partner,
                ).wait_recv()
            if i == 0:
                near = jnp.where(left >= 1, zrecv[way, 0, 0:1], -1.0)
                far = jnp.where(left >= 2, zrecv[way, 1, 0:1], -2.0)
                edge[way] = near
            span = jnp.exp(-own_rates[i] * (2 * BLK))
            row_span = jnp.exp(-own_rates[i] * (2 * BLK * ROW)) * (near == far).astype(F32)
            rows = slice(8 + i * width, 8 + (i + 1) * width)
            entering = jnp.where(left >= 1, zrecv[way, 0, rows] + row_span * zrecv[way, 1, rows], 0.0)
            keep = jnp.ones((1, DH), F32)
            before = near
            for n in range(ROW):
                j = order[n]
                if n == 0:
                    slices[way, i, j] = entering
                else:
                    slices[way, i, j] = slices[way, i, j] + keep * entering
                here = end_of(way, j)
                keep = keep * span * (here == before).astype(F32)
                before = here
            mine = pl.ds(pl.multiple_of(y * width, width), width)
            raw[way, i, mine] = slices[way, i, y]
            for n, j in enumerate(in_row):
                sends.append(
                    copy(
                        slices.at[way, i, j],
                        raw.at[way, i, mine],
                        b_send.at[way, i, n],
                        b_recv.at[way, i, y],
                        at(z, j, c),
                    )
                )
                sends[-1].start()

    to_chips(0)
    to_chips(1)

    beside = []
    for way in (0, 1):
        neighbour = rmeta[(y + ROW - 1) % ROW, 1:2, :] if way == 0 else rmeta[(y + 1) % ROW, 0:1, :]
        beside.append(jnp.where(y == (0 if way == 0 else ROW - 1), edge[way], neighbour))

    def to_core(way):
        inner = lasts[0] if way == 0 else firsts[1]
        kept = (inner == beside[way]).astype(F32)
        for i in range(OWN):
            for j in in_row:
                theirs = pl.ds(pl.multiple_of(j * width, width), width)
                copy(
                    slices.at[way, i, j], raw.at[way, i, theirs], b_send.at[way, i, 0], b_recv.at[way, i, j], partner
                ).wait_recv()
            outer = raw[way, i]
            between = jnp.where(c == way, local[way, OWN * c + i], part[way, i])
            inside = between + jnp.exp(-own_rates[i] * BLK) * kept * outer
            state[way, OWN * c + i] = jnp.where(c == way, outer, inside)
            give[way, i] = jnp.where(c == way, inside, outer)
            sends.append(
                copy(
                    give.at[way, i],
                    state.at[way, OWN * c + i],
                    e_send.at[way, i],
                    e_recv.at[way, i],
                    partner,
                )
            )
            sends[-1].start()

    def from_core(way):
        for i in range(OWN):
            copy(
                give.at[way, i], state.at[way, OWN * (1 - c) + i], e_send.at[way, i], e_recv.at[way, i], partner
            ).wait_recv()

    to_core(0)
    from_core(0)

    seg_before = jnp.where(c == 0, beside[0], lasts[0])
    seg_after = jnp.where(c == 1, beside[1], firsts[1])
    joins = (seg_cols == seg_before).astype(F32)
    leaves = (seg_cols == seg_after).astype(F32)

    squares = None
    for h in range(NH):
        inflow = jnp.exp(-rates[h] * (place + 1.0)) * joins
        high, low = split(state[0, h])
        qh = q[:, cols[h]]
        whole = out[:, cols[h]] + inflow * (dot(qh, high, NN) + dot(qh, low, NN))
        out[:, cols[h]] = whole
        squares = whole * whole if h == 0 else squares + whole * whole
    mine = jnp.broadcast_to(jnp.sum(squares.T, axis=0, keepdims=True), (8, DH))
    xsend[...] = mine
    xrecv[x] = mine
    for n in range(1, xs):
        sends.append(copy(xsend, xrecv.at[x], x_send.at[n - 1], x_recv.at[x], (s, (x + n) % xs)))
        sends[-1].start()

    to_core(1)
    for h in range(NH):
        inflow = jnp.exp(-rates[h] * (place + 1.0)) * joins
        high, low = split(state[0, h])
        gh = g[:, cols[h]]
        dq[:, cols[h]] = dq[:, cols[h]] + inflow * (dot(gh, high, NT) + dot(gh, low, NT))
    from_core(1)
    for h in range(NH):
        outflow = jnp.exp(-rates[h] * (BLK - place)) * leaves
        high, low = split(state[1, h])
        kh, vh = k[:, cols[h]], v[:, cols[h]]
        dk[:, cols[h]] = dk[:, cols[h]] + outflow * (dot(vh, high, NT) + dot(vh, low, NT))
        dv[:, cols[h]] = dv[:, cols[h]] + outflow * (dot(kh, high, NN) + dot(kh, low, NN))

    for n in range(1, xs):
        from_x = (x + n) % xs
        copy(xsend, xrecv.at[from_x], x_send.at[n - 1], x_recv.at[from_x], partner).wait_recv()
    summed = xrecv[0]
    for n in range(1, xs):
        summed = summed + xrecv[n]
    inverse = lax.rsqrt(summed / (NH * DH * xs) + EPSILON)
    scale = jnp.broadcast_to(inverse[0:1, :], (BLK, BLK)).T
    for h in range(NH):
        normed[:, cols[h]] = out[:, cols[h]] * scale * gain[:, cols[h]]

    for sent in sends:
        sent.wait_send()


def body(zs, xs, queries, keys, values, d_out, segment_ids, decay_exps, gain):
    width = BLK // ROW
    vmem = pl.BlockSpec(memory_space=pltpu.VMEM)
    dma = pltpu.SemaphoreType.DMA
    result = jax.ShapeDtypeStruct((BLK, NH * DH), F32)
    return pl.pallas_call(
        functools.partial(kernel, zs, xs),
        out_shape=(result,) * 4,
        in_specs=[pl.BlockSpec(memory_space=pltpu.SMEM)] + [vmem] * 6,
        out_specs=(vmem,) * 4,
        scratch_shapes=[
            pltpu.VMEM((2, NH, DH, DH), F32),
            pltpu.VMEM((2, OWN, DH, DH), F32),
            pltpu.VMEM((8, DH), F32),
            pltpu.VMEM((8, DH), F32),
            pltpu.VMEM((2, OWN, DH, DH), F32),
            pltpu.VMEM((8, DH), F32),
            pltpu.VMEM((ROW, 8, DH), F32),
            pltpu.VMEM((2, OWN, ROW, width, DH), F32),
            pltpu.VMEM((2, 8 + OWN * width, DH), F32),
            pltpu.VMEM((2, 2, 8 + OWN * width, DH), F32),
            pltpu.VMEM((2, OWN, ROW, width, DH), F32),
            pltpu.VMEM((2, OWN, DH, DH), F32),
            pltpu.VMEM((2, OWN, DH, DH), F32),
            pltpu.VMEM((2, NH, DH, DH), F32),
            pltpu.VMEM((BLK, NH * DH), F32),
            pltpu.VMEM((8, DH), F32),
            pltpu.VMEM((xs, 8, DH), F32),
            dma((2, OWN)), dma((2, OWN)),
            dma((1 + ROW,)), dma((1 + ROW,)),
            dma((2, OWN, ROW)), dma((2, OWN, ROW)),
            dma((2, 2, OWN)), dma((2, 2, OWN)),
            dma((2, OWN, ROW)), dma((2, OWN, ROW)),
            dma((2, OWN)), dma((2, OWN)),
            dma((xs,)), dma((xs,)),
        ],
        compiler_params=pltpu.CompilerParams(
            collective_id=0, has_side_effects=True, vmem_limit_bytes=32 << 20
        ),
        name="attention",
    )(decay_exps, segment_ids.reshape(1, BLK), queries, keys, values, d_out, gain.reshape(1, NH * DH))


def solution(mesh):
    both = P("seq", "head")
    return jax.shard_map(
        functools.partial(body, mesh.shape["seq"] // (2 * ROW), mesh.shape["head"]),
        mesh=mesh,
        in_specs=(both, both, both, both, P("seq"), P("head"), P("head")),
        out_specs=(both, both, both, both),
        check_vma=False,
    )
```

time: 1810 us -> 57.1 us (0.03)
  loops' own time: 766 us -> 0 us
  local copies, waits for them, and re-layouts: 303 us -> 7.09 us
  other arithmetic: 281 us -> 0 us
  blocking collectives: 278 us -> 0 us
  waiting for transfers between devices: 141 us -> 0 us
  Pallas kernels: 0 us -> 49.1 us
    another operation x2 -> x0, loops' own time: 766 us -> none  [entering(): return lax.fori_loop(0, size, hop, start)]
    dynamic_slice x512 -> x0, local copies, waits for them, and re-layouts: 292 us -> none  [hop(): new = combine(before, jax.tree.map(lambda part: part[at], everything))]
    select_n x256 -> x0, other arithmetic: 274 us -> none  [hop(): return jax.tree.map(lambda a, b: jnp.where(reached, a, b), new, before)]
    unnamed x1 -> x0, blocking collectives: 264 us -> none
    all_gather x2 -> x0, waiting for transfers between devices: 141 us -> none  [entering(): everything = jax.tree.map(lambda part: lax.all_gather(part, axis), array)]
    pallas_call x0 -> x1, Pallas kernels: none -> 49.1 us  [body(): pl.pallas_call(functools.partial(kernel, zs, xs), out_shape=(result,) * 4...]
  transfers between devices with their start and end apart: 2 -> 0, of which waited for: 1 -> 0; matrix products, arithmetic and copies ran while one was open for 0% -> 0% of each run, Pallas kernels for 0% -> 0%
where the time goes in v1:
time: 57.1 us; the launch traced here: 56.9 us
  Pallas kernels  49.1 us (86%)
  local copies, waits for them, and re-layouts  7.09 us (12%)
  between operations  0.67 us (1%)
    pallas_call x1, Pallas kernels, body(): pl.pallas_call(functools.partial(kernel, zs, xs), out_shape=(result,) * 4...  49.1 us
    unnamed x18, local copies, waits for them, and re-layouts  7.09 us

profile of v1, /device:TPU:1, one launch (start us, length us, event | category | flops | bytes accessed | tf_op | source)
XLA Modules:
  0.0 56.9 jit_solution(3986826839824358681)
XLA Ops:
  0.6 0.0 copy-start.4
  0.6 0.0 copy-start.5
  0.7 0.0 copy-start.6
  0.7 0.7 %copy-done.4 = f32[512]{0:T(512)S(1)} copy-done((f32[512]{0:T(512)S(1)}, f32[512]{0:T(512)}, u32[]{:S(2)}) %copy-start.4) | copy-done | bytes 2072
  1.3 0.0 copy-done.5
  1.3 0.0 copy-done.6
  1.3 0.0 copy-start
  1.3 0.9 %copy-done = bf16[128,512]{1,0:T(8,128)(2,1)S(1)} copy-done((bf16[128,512]{1,0:T(8,128)(2,1)S(1)}, bf16[128,512]{1,0:T(8,128)(2,1)}, u32[]{:S(2)}) %copy-start) | copy-done | bytes 131096
  2.2 0.0 copy-start.1
  2.2 0.9 %copy-done.1 = bf16[128,512]{1,0:T(8,128)(2,1)S(1)} copy-done((bf16[128,512]{1,0:T(8,128)(2,1)S(1)}, bf16[128,512]{1,0:T(8,128)(2,1)}, u32[]{:S(2)}) %copy-start.1) | copy-done | bytes 131096
  3.1 0.0 copy-start.2
  3.1 0.9 %copy-done.2 = bf16[128,512]{1,0:T(8,128)(2,1)S(1)} copy-done((bf16[128,512]{1,0:T(8,128)(2,1)S(1)}, bf16[128,512]{1,0:T(8,128)(2,1)}, u32[]{:S(2)}) %copy-start.2) | copy-done | bytes 131096
  4.0 0.0 copy-start.3
  4.0 0.9 %copy-done.3 = bf16[128,512]{1,0:T(8,128)(2,1)S(1)} copy-done((bf16[128,512]{1,0:T(8,128)(2,1)S(1)}, bf16[128,512]{1,0:T(8,128)(2,1)}, u32[]{:S(2)}) %copy-start.3) | copy-done | bytes 131096
  4.9 49.1 %attention.1 = (f32[128,512]{1,0:T(8,128)S(1)}, f32[128,512]{1,0:T(8,128)S(1)}, f32[128,512]{1,0:T(8,128)S(1)}, f32[128,512]{1,0:T(8,128)S(1)}) custom-call(s32[4]{0:T(128)S(1)} %copy-done.5, s32[1,128]{1,0:T(1,128)S(1)} %bitcast.3, bf16[128,512]{1,0:T(8,128)(2,1)S(1)} %copy-done, bf16[128,512]{1,0:T(8,128)(2,1)S(1)} %copy-done.1, ...), custom_call_target="tpu_custom_call" | custom-call | tf_op jit(solution)/shard_map/attention/pallas_call | solution.py:353
  54.1 0.7 %copy.15 = f32[128,512]{1,0:T(8,128)} copy(f32[128,512]{1,0:T(8,128)S(1)} %get-tuple-element.8) | data formatting | bytes 524288
  54.8 0.7 %copy.16 = f32[128,512]{1,0:T(8,128)} copy(f32[128,512]{1,0:T(8,128)S(1)} %get-tuple-element.9) | data formatting | bytes 524288
  55.5 0.7 %copy.17 = f32[128,512]{1,0:T(8,128)} copy(f32[128,512]{1,0:T(8,128)S(1)} %get-tuple-element.10) | data formatting | bytes 524288
  56.2 0.7 %copy.18 = f32[128,512]{1,0:T(8,128)} copy(f32[128,512]{1,0:T(8,128)S(1)} %get-tuple-element.11) | data formatting | bytes 524288
Async XLA Ops:
  0.6 0.7 %copy-start.4 = (f32[512]{0:T(512)S(1)}, f32[512]{0:T(512)}, u32[]{:S(2)}) copy-start(f32[512]{0:T(512)} %param.13) | copy-start | bytes 6148
  0.6 0.7 %copy-start.5 = (s32[4]{0:T(128)S(1)}, s32[4]{0:T(128)}, u32[]{:S(2)}) copy-start(s32[4]{0:T(128)} %exps.1) | copy-start | bytes 52
  0.7 0.7 %copy-start.6 = (s32[128]{0:T(128)S(1)}, s32[128]{0:T(128)}, u32[]{:S(2)}) copy-start(s32[128]{0:T(128)} %param.11) | copy-start | bytes 1540
  1.3 0.9 %copy-start = (bf16[128,512]{1,0:T(8,128)(2,1)S(1)}, bf16[128,512]{1,0:T(8,128)(2,1)}, u32[]{:S(2)}) copy-start(bf16[128,512]{1,0:T(8,128)(2,1)} %q.1) | copy-start | bytes 393220
  2.2 0.9 %copy-start.1 = (bf16[128,512]{1,0:T(8,128)(2,1)S(1)}, bf16[128,512]{1,0:T(8,128)(2,1)}, u32[]{:S(2)}) copy-start(bf16[128,512]{1,0:T(8,128)(2,1)} %k.1) | copy-start | bytes 393220
  3.1 0.9 %copy-start.2 = (bf16[128,512]{1,0:T(8,128)(2,1)S(1)}, bf16[128,512]{1,0:T(8,128)(2,1)}, u32[]{:S(2)}) copy-start(bf16[128,512]{1,0:T(8,128)(2,1)} %v.1) | copy-start | bytes 393220
  4.0 0.9 %copy-start.3 = (bf16[128,512]{1,0:T(8,128)(2,1)S(1)}, bf16[128,512]{1,0:T(8,128)(2,1)}, u32[]{:S(2)}) copy-start(bf16[128,512]{1,0:T(8,128)(2,1)} %g.1) | copy-start | bytes 393220

commit v2 on v1

--- a/solution.py
+++ b/solution.py
@@ -32,10 +32,11 @@
 
 
 def kernel(
-    zs, xs, exps, seg, q, k, v, g, gain,
+    zs, xs, exps_in, seg_in, q_in, k_in, v_in, g_in, gain_in,
     normed, dq, dk, dv,
+    exps, seg, q, k, v, g, gain,
     local, part, mymeta, pmeta, chip, cmeta, rmeta, there, zsend, zrecv, slices, raw, give, state, out, xsend, xrecv,
-    d_send, d_recv, m_send, m_recv, t_send, t_recv, z_send, z_recv, b_send, b_recv, e_send, e_recv, x_send, x_recv,
+    loads, d_send, d_recv, m_send, m_recv, t_send, t_recv, z_send, z_recv, b_send, b_recv, e_send, e_recv, x_send, x_recv,
 ):
     s, x = lax.axis_index("seq"), lax.axis_index("head")
     c, y, z = s % 2, (s // 2) % ROW, s // (2 * ROW)
@@ -56,11 +57,40 @@
             src_ref=src, dst_ref=dst, send_sem=send, recv_sem=recv, device_id=device, device_id_type=MESH
         )
 
+    def after(way):
+        return zs - 1 - z if way == 0 else z
+
+    def before(way):
+        return after(1 - way)
+
     barrier = pltpu.get_barrier_semaphore()
-    others = [partner] + [at(z, j, c) for j in in_row] + [hop(w, n) for w in (0, 1) for n in (1, 2)]
-    others += [(s, (x + n) % xs) for n in range(1, xs)]
+    others = [partner] + [at(z, j, c) for j in in_row] + [(s, (x + n) % xs) for n in range(1, xs)]
     for device in others:
         pl.semaphore_signal(barrier, inc=1, device_id=device, device_id_type=MESH)
+    hops = [(w, n) for w in (0, 1) for n in (1, 2)]
+    for w, n in hops:
+
+        @pl.when(after(w) >= n)
+        def _():
+            pl.semaphore_signal(barrier, inc=1, device_id=hop(w, n), device_id_type=MESH)
+
+    fetches = [
+        pltpu.make_async_copy(src, dst, loads.at[n])
+        for n, (src, dst) in enumerate(
+            [(seg_in, seg), (exps_in, exps), (k_in, k), (v_in, v), (q_in, q), (g_in, g), (gain_in, gain)]
+        )
+    ]
+    for fetch in fetches:
+        fetch.start()
+    for w, n in hops:
+
+        @pl.when(before(w) < n)
+        def _():
+            zrecv[w, n - 1, 0:8] = jnp.full((8, DH), -float(n), F32)
+            zrecv[w, n - 1, 8:] = jnp.zeros((OWN * width, DH), F32)
+
+    for fetch in fetches[:4]:
+        fetch.wait()
 
     place = lax.broadcasted_iota(jnp.int32, (BLK, DH), 0).astype(F32)
     seg_row = seg[...].astype(F32)
@@ -89,7 +119,7 @@
         weight = jnp.exp(-rates[h] * (BLK - 1.0 - place)) * ends
         local[0, h] = weighted(weight, k[:, cols[h]], v[:, cols[h]])
 
-    pl.semaphore_wait(barrier, len(others))
+    pl.semaphore_wait(barrier, len(others) + jnp.minimum(z, 2) + jnp.minimum(zs - 1 - z, 2))
 
     meta_copy = copy(mymeta, pmeta, m_send.at[0], m_recv.at[0], partner)
     meta_copy.start()
@@ -106,6 +136,8 @@
         return found
 
     first_copies = [to_partner(0)]
+    for fetch in fetches[4:]:
+        fetch.wait()
     for h in range(NH):
         weight = jnp.exp(-rates[h] * place) * starts
         local[1, h] = weighted(weight, q[:, cols[h]], g[:, cols[h]])
@@ -171,6 +203,12 @@
     def end_of(way, j):
         return rmeta[j, 1:2, :] if way == 0 else rmeta[j, 0:1, :]
 
+    def z_copy(way, n, i):
+        rows = slice(0, 8 + width) if i == 0 else slice(8 + width, 8 + 2 * width)
+        return copy(
+            zsend.at[way, rows], zrecv.at[way, n - 1, rows], z_send.at[way, n - 1, i], z_recv.at[way, n - 1, i], hop(way, n)
+        )
+
     orders = [list(range(ROW)), list(range(ROW))[::-1]]
 
     def to_rows(way):
@@ -187,19 +225,11 @@
                 slices[way, i, order[n]] = sofar
                 keep = span * (end_of(way, order[n]) == end_of(way, order[n - 1])).astype(F32)
                 sofar = there[way, i, order[n]] + keep * sofar
-            low, high = (0, 8 + width) if i == 0 else (8 + width, 8 + 2 * width)
             zsend[way, 8 + i * width : 8 + (i + 1) * width] = sofar
             for n in (1, 2):
-                sends.append(
-                    copy(
-                        zsend.at[way, low:high],
-                        zrecv.at[way, n - 1, low:high],
-                        z_send.at[way, n - 1, i],
-                        z_recv.at[way, n - 1, i],
-                        hop(way, n),
-                    )
-                )
-                sends[-1].start()
+                @pl.when(after(way) >= n)
+                def _():
+                    z_copy(way, n, i).start()
 
     to_rows(0)
     to_rows(1)
@@ -210,27 +240,22 @@
 
     def to_chips(way):
         order = orders[way]
-        left = z if way == 0 else zs - 1 - z
-        for i in range(OWN):
-            low, high = (0, 8 + width) if i == 0 else (8 + width, 8 + 2 * width)
+        for i in range(OWN):
             for n in (1, 2):
-                copy(
-                    zsend.at[way, low:high],
-                    zrecv.at[way, n - 1, low:high],
-                    z_send.at[way, n - 1, i],
-                    z_recv.at[way, n - 1, i],
-                    partner,
-                ).wait_recv()
+
+                @pl.when(before(way) >= n)
+                def _():
+                    z_copy(way, n, i).wait_recv()
+
             if i == 0:
-                near = jnp.where(left >= 1, zrecv[way, 0, 0:1], -1.0)
-                far = jnp.where(left >= 2, zrecv[way, 1, 0:1], -2.0)
+                near, far = zrecv[way, 0, 0:1], zrecv[way, 1, 0:1]
                 edge[way] = near
             span = jnp.exp(-own_rates[i] * (2 * BLK))
             row_span = jnp.exp(-own_rates[i] * (2 * BLK * ROW)) * (near == far).astype(F32)
             rows = slice(8 + i * width, 8 + (i + 1) * width)
-            entering = jnp.where(left >= 1, zrecv[way, 0, rows] + row_span * zrecv[way, 1, rows], 0.0)
+            entering = zrecv[way, 0, rows] + row_span * zrecv[way, 1, rows]
             keep = jnp.ones((1, DH), F32)
-            before = near
+            there_end = near
             for n in range(ROW):
                 j = order[n]
                 if n == 0:
@@ -238,8 +263,8 @@
                 else:
                     slices[way, i, j] = slices[way, i, j] + keep * entering
                 here = end_of(way, j)
-                keep = keep * span * (here == before).astype(F32)
-                before = here
+                keep = keep * span * (here == there_end).astype(F32)
+                there_end = here
             mine = pl.ds(pl.multiple_of(y * width, width), width)
             raw[way, i, mine] = slices[way, i, y]
             for n, j in enumerate(in_row):
@@ -343,6 +368,21 @@
 
     for sent in sends:
         sent.wait_send()
+    for w, n in hops:
+        for i in range(OWN):
+
+            @pl.when(after(w) >= n)
+            def _():
+                z_copy(w, n, i).wait_send()
+
+
+def finish(*refs):
+    sems = refs[8]
+    stores = [pltpu.make_async_copy(refs[n], refs[4 + n], sems.at[n]) for n in range(4)]
+    for store in stores:
+        store.start()
+    for store in stores:
+        store.wait()
 
 
 def body(zs, xs, queries, keys, values, d_out, segment_ids, decay_exps, gain):
@@ -350,12 +390,19 @@
     vmem = pl.BlockSpec(memory_space=pltpu.VMEM)
     dma = pltpu.SemaphoreType.DMA
     result = jax.ShapeDtypeStruct((BLK, NH * DH), F32)
-    return pl.pallas_call(
+    operands = (
+        decay_exps, segment_ids.reshape(1, BLK), queries, keys, values, d_out, gain.reshape(1, NH * DH)
+    )
+    held = pl.pallas_call(
         functools.partial(kernel, zs, xs),
         out_shape=(result,) * 4,
-        in_specs=[pl.BlockSpec(memory_space=pltpu.SMEM)] + [vmem] * 6,
+        in_specs=[pl.BlockSpec(memory_space=pltpu.HBM)] * 7,
         out_specs=(vmem,) * 4,
         scratch_shapes=[
+            pltpu.SMEM((NH,), jnp.int32),
+            pltpu.VMEM((1, BLK), jnp.int32),
+            *[pltpu.VMEM((BLK, NH * DH), BF16)] * 4,
+            pltpu.VMEM((1, NH * DH), F32),
             pltpu.VMEM((2, NH, DH, DH), F32),
             pltpu.VMEM((2, OWN, DH, DH), F32),
             pltpu.VMEM((8, DH), F32),
@@ -373,6 +420,7 @@
             pltpu.VMEM((BLK, NH * DH), F32),
             pltpu.VMEM((8, DH), F32),
             pltpu.VMEM((xs, 8, DH), F32),
+            dma((7,)),
             dma((2, OWN)), dma((2, OWN)),
             dma((1 + ROW,)), dma((1 + ROW,)),
             dma((2, OWN, ROW)), dma((2, OWN, ROW)),
@@ -385,7 +433,15 @@
             collective_id=0, has_side_effects=True, vmem_limit_bytes=32 << 20
         ),
         name="attention",
-    )(decay_exps, segment_ids.reshape(1, BLK), queries, keys, values, d_out, gain.reshape(1, NH * DH))
+    )(*(pltpu.with_memory_space_constraint(operand, pltpu.HBM) for operand in operands))
+    return pl.pallas_call(
+        finish,
+        out_shape=(result,) * 4,
+        in_specs=[vmem] * 4,
+        out_specs=(pl.BlockSpec(memory_space=pl.ANY),) * 4,
+        scratch_shapes=[dma((4,))],
+        name="finish",
+    )(*(pltpu.with_memory_space_constraint(part, pltpu.VMEM) for part in held))
 
 
 def solution(mesh):

time: 57.1 us -> 44 us (0.77)
  local copies, waits for them, and re-layouts: 7.09 us -> 0 us
  Pallas kernels: 49.1 us -> 43.2 us
    unnamed x18 -> x0, local copies, waits for them, and re-layouts: 7.09 us -> none
    pallas_call x1, Pallas kernels: 49.1 us -> 42.2 us  [body(): pl.pallas_call(functools.partial(kernel, zs, xs), out_shape=(result,) * 4...]
    pallas_call x0 -> x1, Pallas kernels: none -> 1 us  [body(): pl.pallas_call(finish, out_shape=(result,) * 4, in_specs=[vmem] * 4, out_...]
where the time goes in v2:
time: 44 us; the launch traced here: 43.8 us
  Pallas kernels  43.2 us (98%)
  between operations  0.64 us (1%)
    pallas_call x1, Pallas kernels, body(): pl.pallas_call(functools.partial(kernel, zs, xs), out_shape=(result,) * 4...  42.2 us
    pallas_call x1, Pallas kernels, body(): pl.pallas_call(finish, out_shape=(result,) * 4, in_specs=[vmem] * 4, out_...  1 us

profile of v2, /device:TPU:1, one launch (start us, length us, event | category | flops | bytes accessed | tf_op | source)
XLA Modules:
  0.0 43.8 jit_solution(17686588475621826525)
XLA Ops:
  0.6 42.2 %attention.1 = (f32[128,512]{1,0:T(8,128)S(1)}, f32[128,512]{1,0:T(8,128)S(1)}, f32[128,512]{1,0:T(8,128)S(1)}, f32[128,512]{1,0:T(8,128)S(1)}) custom-call(s32[4]{0:T(128)} %exps_in.1, s32[1,128]{1,0:T(1,128)} %bitcast.3, bf16[128,512]{1,0:T(8,128)(2,1)} %q_in.1, bf16[128,512]{1,0:T(8,128)(2,1)} %k_in.1, bf16[128,512]{1,0:T(8,128)(2,1)} %v_in.1, ...), custom_call_target="tpu_custom_call" | custom-call | tf_op jit(solution)/shard_map/attention/pallas_call | solution.py:396
  42.8 1.0 %finish.1 = (f32[128,512]{1,0:T(8,128)}, f32[128,512]{1,0:T(8,128)}, f32[128,512]{1,0:T(8,128)}, f32[128,512]{1,0:T(8,128)}) custom-call(f32[128,512]{1,0:T(8,128)S(1)} %get-tuple-element.8.refs_0_, f32[128,512]{1,0:T(8,128)S(1)} %get-tuple-element.9.refs_1_, f32[128,512]{1,0:T(8,128)S(1)} %get-tuple-element.10.refs_2_, f32[128,512]{1,0:T(8,128)S(1)} %get-tuple-element.11.refs_3_), custom_call_target="tpu_custom_call" | custom-call | tf_op jit(solution)/shard_map/finish/pallas_call | solution.py:437

commit v3 on v2

v3 whole, which is shorter than its diff:
```python
import functools

import jax
import jax.numpy as jnp
from jax import lax
from jax.experimental import pallas as pl
from jax.experimental.pallas import tpu as pltpu
from jax.sharding import PartitionSpec as P

DH = 128
BLK = 128
NH = 4
OWN = 2
ROW = 8
PIECES = 1
EPSILON = 1e-06
MESH = pl.DeviceIdType.MESH
F32 = jnp.float32
BF16 = jnp.bfloat16

NN = (((1,), (0,)), ((), ()))
NT = (((1,), (1,)), ((), ()))
TN = (((0,), (0,)), ((), ()))


def dot(a, b, dims):
    return lax.dot_general(a, b, dims, preferred_element_type=F32)


def split(a):
    high = a.astype(BF16)
    return high, (a - high.astype(F32)).astype(BF16)


def kernel(
    zs, xs, exps_in, seg_in, q_in, k_in, v_in, g_in, gain_in,
    normed, dq, dk, dv,
    exps, seg, q, k, v, g, gain,
    local, part, mymeta, pmeta, chip, cmeta, rmeta, there, zsend, zrecv, slices, raw, give, state, out, inw, outw,
    given, got, pout, outgot, xsend, xrecv,
    loads, g_send, g_recv, o_send, o_recv, d_send, d_recv, m_send, m_recv, t_send, t_recv, z_send, z_recv, b_send, b_recv, e_send, e_recv, x_send, x_recv,
):
    s, x = lax.axis_index("seq"), lax.axis_index("head")
    c, y, z = s % 2, (s // 2) % ROW, s // (2 * ROW)
    width = BLK // ROW
    total_tokens = BLK * 2 * ROW * zs

    def at(zz, yy, cc):
        return ((zz * ROW + yy) * 2 + cc, x)

    partner = at(z, y, 1 - c)
    far_first = sorted(range(1, ROW), key=lambda n: -min(n, ROW - n))
    in_row = [(y + n) % ROW for n in far_first]
    x_first = sorted(range(1, xs), key=lambda n: -min(n, xs - n))

    def hop(way, n):
        return at((z + (n if way == 0 else zs - n)) % zs, y, c)

    def copy(src, dst, send, recv, device):
        return pltpu.make_async_remote_copy(
            src_ref=src, dst_ref=dst, send_sem=send, recv_sem=recv, device_id=device, device_id_type=MESH
        )

    def after(way):
        return zs - 1 - z if way == 0 else z

    def before(way):
        return after(1 - way)

    halves = [pl.ds(pl.multiple_of(OWN * DH * n, OWN * DH), OWN * DH) for n in (1 - c, c)]
    fetches = [
        pltpu.make_async_copy(src, dst, loads.at[n])
        for n, (src, dst) in enumerate(
            [(seg_in, seg), (exps_in, exps)]
            + [(ref.at[:, half], to.at[:, half]) for half in halves for ref, to in ((k_in, k), (v_in, v))]
            + [(q_in, q), (g_in, g), (gain_in, gain)]
        )
    ]
    for fetch in fetches:
        fetch.start()
    barrier = pltpu.get_barrier_semaphore()
    others = [at(z, j, c) for j in in_row] + [(s, (x + n) % xs) for n in x_first]
    others += [(partner[0], (x + n) % xs) for n in x_first] + [partner]
    for device in others:
        pl.semaphore_signal(barrier, inc=1, device_id=device, device_id_type=MESH)
    hops = [(w, n) for w in (0, 1) for n in (1, 2)]
    for w, n in hops:

        @pl.when(after(w) >= n)
        def _():
            pl.semaphore_signal(barrier, inc=1, device_id=hop(w, n), device_id_type=MESH)

    for w, n in hops:

        @pl.when(before(w) < n)
        def _():
            zrecv[w, n - 1, 0:8] = jnp.full((8, DH), -float(n), F32)
            zrecv[w, n - 1, 8:] = jnp.zeros((OWN * width, DH), F32)

    for fetch in fetches[:2]:
        fetch.wait()

    place = lax.broadcasted_iota(jnp.int32, (BLK, DH), 0).astype(F32)
    seg_row = seg[...].astype(F32)
    seg_rows = jnp.broadcast_to(seg_row, (BLK, BLK))
    seg_cols = seg_rows.T
    first = jnp.broadcast_to(seg_cols[0:1, :], (8, DH))
    last = jnp.broadcast_to(seg_cols[BLK - 1 : BLK, :], (8, DH))
    row_id = lax.broadcasted_iota(jnp.int32, (8, DH), 0)
    mymeta[...] = jnp.where(row_id == 0, first, jnp.where(row_id == 1, last, seg_rows[0:8]))

    def rate_of(h):
        whole = jnp.left_shift(jnp.ones((1, DH), jnp.int32), jnp.full((1, DH), exps[h], jnp.int32))
        return whole.astype(F32) / total_tokens

    rates = [rate_of(h) for h in range(NH)]
    own_rates = [rate_of(OWN * c + i) for i in range(OWN)]
    cols = [slice(h * DH, (h + 1) * DH) for h in range(NH)]

    def weighted(weight, left, right):
        high, low = split(weight * left.astype(F32))
        return dot(high, right, TN) + dot(low, right, TN)

    ends = (seg_cols == last[0:1, :]).astype(F32)
    starts = (seg_cols == first[0:1, :]).astype(F32)
    mine = [OWN * c + i for i in range(OWN)]
    theirs = [OWN * (1 - c) + i for i in range(OWN)]
    their_rates = [rate_of(h) for h in theirs]

    def columns(h):
        return pl.ds(pl.multiple_of(h * DH, DH), DH)

    def local_state(way, h, rate):
        if way == 0:
            weight = jnp.exp(-rate * (BLK - 1.0 - place)) * ends
            local[0, h] = weighted(weight, k[:, columns(h)], v[:, columns(h)])
        else:
            weight = jnp.exp(-rate * place) * starts
            local[1, h] = weighted(weight, q[:, columns(h)], g[:, columns(h)])

    distance = place - lax.broadcasted_iota(jnp.int32, (BLK, DH), 1).astype(F32)
    causal = (distance >= 0) & (seg_cols == seg_rows)
    reach = jnp.maximum(distance, 0.0)

    def within(h):
        decay = jnp.where(causal, jnp.exp(-rates[h] * reach), 0.0)
        qh, kh, vh, gh = q[:, cols[h]], k[:, cols[h]], v[:, cols[h]], g[:, cols[h]]
        scores = (dot(qh, kh, NT) * decay).astype(BF16)
        grad_scores = (dot(gh, vh, NT) * decay).astype(BF16)
        out[:, cols[h]] = dot(scores, vh, NN)
        dq[:, cols[h]] = dot(grad_scores, kh, NN)
        dk[:, cols[h]] = dot(grad_scores, qh, TN)
        dv[:, cols[h]] = dot(scores, gh, TN)

    def in_blocks():
        for h in range(NH):
            within(h)
        given[...] = q[:, halves[0]].astype(F32)

    def wait_for(some):
        for fetch in some:
            fetch.wait()

    def local_states(way, heads, head_rates):
        for h, rate in zip(heads, head_rates):
            local_state(way, h, rate)

    last_out = (s == 0) & (x == 0)

    @pl.when(last_out)
    def _():
        wait_for(fetches[2:4])
        local_states(0, theirs, their_rates)

    @pl.when(jnp.logical_not(last_out))
    def _():
        wait_for(fetches[2:])
        for way in (0, 1):
            local_states(way, theirs, their_rates)
            local_states(way, mine, own_rates)
        in_blocks()

    pl.semaphore_wait(barrier, len(others) + jnp.minimum(z, 2) + jnp.minimum(zs - 1 - z, 2))

    meta_copy = copy(mymeta, pmeta, m_send.at[0], m_recv.at[0], partner)
    meta_copy.start()
    sends = [meta_copy]

    first_copies = [
        [
            copy(local.at[way, theirs[i]], part.at[way, i], d_send.at[way, i], d_recv.at[way, i], partner)
            for i in range(OWN)
        ]
        for way in (0, 1)
    ]
    sends.extend(first_copies[0] + first_copies[1])
    for first_copy in first_copies[0]:
        first_copy.start()

    @pl.when(last_out)
    def _():
        wait_for(fetches[4:6])
        local_states(0, mine, own_rates)

    @pl.when(jnp.logical_not(last_out))
    def _():
        for first_copy in first_copies[1]:
            first_copy.start()


    meta_copy.wait_recv()
    firsts = [jnp.where(c == 0, mymeta[0:1, :], pmeta[0:1, :]), jnp.where(c == 0, pmeta[0:1, :], mymeta[0:1, :])]
    lasts = [jnp.where(c == 0, mymeta[1:2, :], pmeta[1:2, :]), jnp.where(c == 0, pmeta[1:2, :], mymeta[1:2, :])]
    chip_meta = jnp.where(row_id == 0, jnp.broadcast_to(firsts[0], (8, DH)), jnp.broadcast_to(lasts[1], (8, DH)))
    cmeta[...] = chip_meta
    rmeta[y] = chip_meta
    same_chip = [(lasts[0] == lasts[1]).astype(F32), (firsts[0] == firsts[1]).astype(F32)]

    def to_row(way):
        for i in range(OWN):
            first_copies[way][i].wait_recv()
            carried = jnp.exp(-own_rates[i] * BLK) * same_chip[way]
            mine = jnp.where(c == 1 - way, 1.0, carried)
            theirs = jnp.where(c == 1 - way, carried, 1.0)
            whole = mine * local[way, OWN * c + i] + theirs * part[way, i]
            chip[way, i] = whole
            for n, j in enumerate(in_row):
                sends.append(
                    copy(
                        chip.at[way, i, pl.ds(pl.multiple_of(j * width, width), width)],
                        there.at[way, i, y],
                        t_send.at[way, i, n],
                        t_recv.at[way, i, y],
                        at(z, j, c),
                    )
                )
                sends[-1].start()
            there[way, i, y] = chip[way, i, pl.ds(pl.multiple_of(y * width, width), width), :]

    to_row(0)
    for n, j in enumerate(in_row):
        sends.append(copy(cmeta, rmeta.at[y], m_send.at[1 + n], m_recv.at[1 + y], at(z, j, c)))
        sends[-1].start()

    @pl.when(last_out)
    def _():
        wait_for(fetches[6:])
        local_states(1, theirs, their_rates)
        for first_copy in first_copies[1]:
            first_copy.start()
        local_states(1, mine, own_rates)


    to_row(1)

    @pl.when(last_out)
    def _():
        in_blocks()

    gifts = [
        copy(given, got.at[0], g_send.at[0], g_recv.at[0], partner),
        copy(out.at[:, halves[0]], got.at[1], g_send.at[1], g_recv.at[1], partner),
    ]
    for gift in gifts:
        gift.start()
    sends.extend(gifts)

    for j in in_row:
        copy(cmeta, rmeta.at[j], m_send.at[0], m_recv.at[1 + j], partner).wait_recv()

    def end_of(way, j):
        return rmeta[j, 1:2, :] if way == 0 else rmeta[j, 0:1, :]

    def z_copy(way, n, i):
        rows = slice(0, 8 + width) if i == 0 else slice(8 + width, 8 + 2 * width)
        return copy(
            zsend.at[way, rows], zrecv.at[way, n - 1, rows], z_send.at[way, n - 1, i], z_recv.at[way, n - 1, i], hop(way, n)
        )

    orders = [list(range(ROW)), list(range(ROW))[::-1]]

    def row_copy(way, i, j):
        return copy(there.at[way, i, y], there.at[way, i, j], t_send.at[way, i, 0], t_recv.at[way, i, j], partner)

    def end_wait(way, i):
        end = orders[way][-1]

        @pl.when(y != end)
        def _():
            row_copy(way, i, end).wait_recv()

    def to_rows(way):
        order = orders[way]
        zsend[way, 0:8] = jnp.broadcast_to(end_of(way, order[-1]), (8, DH))
        for i in range(OWN):
            for j in in_row:

                @pl.when(j != order[-1])
                def _():
                    row_copy(way, i, j).wait_recv()

            span = jnp.exp(-own_rates[i] * (2 * BLK))
            sofar = there[way, i, order[0]]
            for n in range(1, ROW):
                slices[way, i, order[n]] = sofar
                keep = span * (end_of(way, order[n]) == end_of(way, order[n - 1])).astype(F32)
                if n < ROW - 1:
                    sofar = there[way, i, order[n]] + keep * sofar

            @pl.when(after(way) >= 1)
            def _():
                end_wait(way, i)
                zsend[way, 8 + i * width : 8 + (i + 1) * width] = there[way, i, order[-1]] + keep * sofar
                z_copy(way, 1, i).start()

            @pl.when(after(way) >= 2)
            def _():
                z_copy(way, 2, i).start()


    to_rows(0)
    to_rows(1)

    edge = [None, None]

    def to_chips(way):
        order = orders[way]
        for i in range(OWN):
            for n in (1, 2):

                @pl.when(before(way) >= n)
                def _():
                    z_copy(way, n, i).wait_recv()

            if i == 0:
                near, far = zrecv[way, 0, 0:1], zrecv[way, 1, 0:1]
                edge[way] = near
            span = jnp.exp(-own_rates[i] * (2 * BLK))
            row_span = jnp.exp(-own_rates[i] * (2 * BLK * ROW)) * (near == far).astype(F32)
            rows = slice(8 + i * width, 8 + (i + 1) * width)
            entering = zrecv[way, 0, rows] + row_span * zrecv[way, 1, rows]
            keep = jnp.ones((1, DH), F32)
            there_end = near
            for n in range(ROW):
                j = order[n]
                if n == 0:
                    slices[way, i, j] = entering
                else:
                    slices[way, i, j] = slices[way, i, j] + keep * entering
                here = end_of(way, j)
                keep = keep * span * (here == there_end).astype(F32)
                there_end = here
            here = pl.ds(pl.multiple_of(y * width, width), width)
            for n, j in enumerate(in_row):
                sends.append(
                    copy(
                        slices.at[way, i, j],
                        raw.at[way, i, here],
                        b_send.at[way, i, n],
                        b_recv.at[way, i, y],
                        at(z, j, c),
                    )
                )
                sends[-1].start()
            raw[way, i, here] = slices[way, i, y]

    to_chips(0)
    to_chips(1)

    beside = []
    for way in (0, 1):
        neighbour = rmeta[(y + ROW - 1) % ROW, 1:2, :] if way == 0 else rmeta[(y + 1) % ROW, 0:1, :]
        beside.append(jnp.where(y == (0 if way == 0 else ROW - 1), edge[way], neighbour))

    def to_core(way):
        inner = lasts[0] if way == 0 else firsts[1]
        kept = (inner == beside[way]).astype(F32)
        for i in range(OWN):
            for j in in_row:
                there_rows = pl.ds(pl.multiple_of(j * width, width), width)
                copy(
                    slices.at[way, i, j], raw.at[way, i, there_rows], b_send.at[way, i, 0], b_recv.at[way, i, j], partner
                ).wait_recv()
            outer = raw[way, i]
            between = jnp.where(c == way, local[way, OWN * c + i], part[way, i])
            inside = between + jnp.exp(-own_rates[i] * BLK) * kept * outer
            give[way, i] = jnp.where(c == way, inside, outer)
            sends.append(
                copy(
                    give.at[way, i],
                    state.at[way, OWN * c + i],
                    e_send.at[way, i],
                    e_recv.at[way, i],
                    partner,
                )
            )
            sends[-1].start()
            state[way, OWN * c + i] = jnp.where(c == way, outer, inside)

    def from_core(way):
        for i in range(OWN):
            copy(
                give.at[way, i], state.at[way, OWN * (1 - c) + i], e_send.at[way, i], e_recv.at[way, i], partner
            ).wait_recv()

    seg_before = jnp.where(c == 0, beside[0], lasts[0])
    seg_after = jnp.where(c == 1, beside[1], firsts[1])
    joins = (seg_cols == seg_before).astype(F32)
    leaves = (seg_cols == seg_after).astype(F32)
    partner_cols = jnp.broadcast_to(pmeta[2:3, :], (BLK, BLK)).T
    partner_joins = (partner_cols == jnp.where(c == 1, beside[0], lasts[0])).astype(F32)
    for i in range(OWN):
        weight = jnp.exp(-own_rates[i] * (place + 1.0))
        inw[0, i] = weight * joins
        inw[1, i] = weight * partner_joins
        inw[2, i] = jnp.exp(-their_rates[i] * (place + 1.0)) * joins
        outw[0, i] = jnp.exp(-own_rates[i] * (BLK - place)) * leaves
        outw[1, i] = jnp.exp(-their_rates[i] * (BLK - place)) * leaves
    for gift in gifts:
        gift.wait_recv()

    to_core(0)

    def output(within_out, query, entering, weight):
        high, low = split(entering)
        return within_out + weight * (dot(query, high, NN) + dot(query, low, NN))

    squares, partner_squares = jnp.zeros((BLK, DH), F32), jnp.zeros((BLK, DH), F32)
    for i in range(OWN):
        whole = output(got[1, :, cols[i]], got[0, :, cols[i]].astype(BF16), give[0, i], inw[1, i])
        pout[:, cols[i]] = whole
        partner_squares = partner_squares + whole * whole
        at_mine = columns(mine[i])
        whole = output(out[:, at_mine], q[:, at_mine], state[0, mine[i]], inw[0, i])
        out[:, at_mine] = whole
        squares = squares + whole * whole

    def row_of(total):
        return jnp.broadcast_to(jnp.sum(total.T, axis=0, keepdims=True), (8, DH))

    xsend[0] = row_of(squares)
    xsend[1] = row_of(partner_squares)
    last_sends = [
        copy(xsend.at[m], xrecv.at[c, x], x_send.at[m, n], x_recv.at[c, x], (to, (x + n) % xs))
        for n in x_first
        for m, to in ((0, s), (1, partner[0]))
    ]
    last_sends.append(copy(xsend.at[1], xrecv.at[c, x], x_send.at[1, 0], x_recv.at[c, x], partner))
    for sent in last_sends:
        sent.start()
    out_copy = copy(pout, outgot, o_send.at[0], o_recv.at[0], partner)
    out_copy.start()
    sends.append(out_copy)
    xrecv[c, x] = xsend[0]

    to_core(1)

    def grad_query(h, inflow):
        high, low = split(state[0, h])
        gh = g[:, columns(h)]
        dq[:, columns(h)] = dq[:, columns(h)] + inflow * (dot(gh, high, NT) + dot(gh, low, NT))

    def grad_key_value(h, outflow):
        high, low = split(state[1, h])
        kh, vh = k[:, columns(h)], v[:, columns(h)]
        dk[:, columns(h)] = dk[:, columns(h)] + outflow * (dot(vh, high, NT) + dot(vh, low, NT))
        dv[:, columns(h)] = dv[:, columns(h)] + outflow * (dot(kh, high, NN) + dot(kh, low, NN))

    for i in range(OWN):
        grad_key_value(mine[i], outw[0, i])
        grad_query(mine[i], inw[0, i])
    from_core(0)
    for i in range(OWN):
        grad_query(theirs[i], inw[2, i])
    from_core(1)
    for i in range(OWN):
        grad_key_value(theirs[i], outw[1, i])

    for way in (0, 1):

        @pl.when(after(way) < 1)
        def _():
            for i in range(OWN):
                end_wait(way, i)

    out_copy.wait_recv()
    for sent in sends:
        sent.wait_send()
    for w, n in hops:
        for i in range(OWN):

            @pl.when(after(w) >= n)
            def _():
                z_copy(w, n, i).wait_send()

    for m in (c, 1 - c):
        for n in (x_first if m is c else [*x_first, 0]):
            from_x = (x + n) % xs
            copy(xsend.at[0], xrecv.at[m, from_x], x_send.at[0, n], x_recv.at[m, from_x], partner).wait_recv()
    summed = xrecv[0, 0] + xrecv[1, 0]
    for n in range(1, xs):
        summed = summed + (xrecv[0, n] + xrecv[1, n])
    inverse = lax.rsqrt(summed / (NH * DH * xs) + EPSILON)
    scale = jnp.broadcast_to(inverse[0:1, :], (BLK, BLK)).T
    for i in range(OWN):
        at_mine, at_theirs = columns(mine[i]), columns(theirs[i])
        normed[:, at_mine] = out[:, at_mine] * gain[:, at_mine] * scale
        normed[:, at_theirs] = outgot[:, cols[i]] * gain[:, at_theirs] * scale
    for sent in last_sends:
        sent.wait_send()


def finish(*refs):
    sems = refs[8]
    rows = [pl.ds(n * BLK // PIECES, BLK // PIECES) for n in range(PIECES)]
    stores = [
        pltpu.make_async_copy(refs[n].at[piece], refs[4 + n].at[piece], sems.at[n, m])
        for n in range(4)
        for m, piece in enumerate(rows)
    ]
    for store in stores:
        store.start()
    for store in stores:
        store.wait()


def body(zs, xs, queries, keys, values, d_out, segment_ids, decay_exps, gain):
    width = BLK // ROW
    vmem = pl.BlockSpec(memory_space=pltpu.VMEM)
    dma = pltpu.SemaphoreType.DMA
    result = jax.ShapeDtypeStruct((BLK, NH * DH), F32)
    operands = (
        decay_exps, segment_ids.reshape(1, BLK), queries, keys, values, d_out, gain.reshape(1, NH * DH)
    )
    held = pl.pallas_call(
        functools.partial(kernel, zs, xs),
        out_shape=(result,) * 4,
        in_specs=[pl.BlockSpec(memory_space=pltpu.HBM)] * 7,
        out_specs=(vmem,) * 4,
        scratch_shapes=[
            pltpu.SMEM((NH,), jnp.int32),
            pltpu.VMEM((1, BLK), jnp.int32),
            *[pltpu.VMEM((BLK, NH * DH), BF16)] * 4,
            pltpu.VMEM((1, NH * DH), F32),
            pltpu.VMEM((2, NH, DH, DH), F32),
            pltpu.VMEM((2, OWN, DH, DH), F32),
            pltpu.VMEM((8, DH), F32),
            pltpu.VMEM((8, DH), F32),
            pltpu.VMEM((2, OWN, DH, DH), F32),
            pltpu.VMEM((8, DH), F32),
            pltpu.VMEM((ROW, 8, DH), F32),
            pltpu.VMEM((2, OWN, ROW, width, DH), F32),
            pltpu.VMEM((2, 8 + OWN * width, DH), F32),
            pltpu.VMEM((2, 2, 8 + OWN * width, DH), F32),
            pltpu.VMEM((2, OWN, ROW, width, DH), F32),
            pltpu.VMEM((2, OWN, DH, DH), F32),
            pltpu.VMEM((2, OWN, DH, DH), F32),
            pltpu.VMEM((2, NH, DH, DH), F32),
            pltpu.VMEM((BLK, NH * DH), F32),
            pltpu.VMEM((3, OWN, BLK, DH), F32),
            pltpu.VMEM((2, OWN, BLK, DH), F32),
            pltpu.VMEM((BLK, OWN * DH), F32),
            pltpu.VMEM((2, BLK, OWN * DH), F32),
            pltpu.VMEM((BLK, OWN * DH), F32),
            pltpu.VMEM((BLK, OWN * DH), F32),
            pltpu.VMEM((2, 8, DH), F32),
            pltpu.VMEM((2, xs, 8, DH), F32),
            dma((9,)),
            dma((2,)), dma((2,)),
            dma((1,)), dma((1,)),
            dma((2, OWN)), dma((2, OWN)),
            dma((1 + ROW,)), dma((1 + ROW,)),
            dma((2, OWN, ROW)), dma((2, OWN, ROW)),
            dma((2, 2, OWN)), dma((2, 2, OWN)),
            dma((2, OWN, ROW)), dma((2, OWN, ROW)),
            dma((2, OWN)), dma((2, OWN)),
            dma((2, xs)), dma((2, xs)),
        ],
        compiler_params=pltpu.CompilerParams(
            collective_id=0, has_side_effects=True, vmem_limit_bytes=32 << 20
        ),
        name="attention",
    )(*(pltpu.with_memory_space_constraint(operand, pltpu.HBM) for operand in operands))
    return pl.pallas_call(
        finish,
        out_shape=(result,) * 4,
        in_specs=[vmem] * 4,
        out_specs=(pl.BlockSpec(memory_space=pl.ANY),) * 4,
        scratch_shapes=[dma((4, PIECES))],
        name="finish",
    )(*(pltpu.with_memory_space_constraint(part, pltpu.VMEM) for part in held))


def solution(mesh):
    both = P("seq", "head")
    return jax.shard_map(
        functools.partial(body, mesh.shape["seq"] // (2 * ROW), mesh.shape["head"]),
        mesh=mesh,
        in_specs=(both, both, both, both, P("seq"), P("head"), P("head")),
        out_specs=(both, both, both, both),
        check_vma=False,
    )
```

time: 44 us -> 42.3 us (0.961)
  Pallas kernels: 43.2 us -> 41.5 us
    pallas_call x1, Pallas kernels: 42.2 us -> 40.5 us  [body(): pl.pallas_call(functools.partial(kernel, zs, xs), out_shape=(result,) * 4...]
where the time goes in v3:
time: 42.3 us; the launch traced here: 42.1 us
  Pallas kernels  41.5 us (98%)
  between operations  0.64 us (2%)
    pallas_call x1, Pallas kernels, body(): pl.pallas_call(functools.partial(kernel, zs, xs), out_shape=(result,) * 4...  40.5 us
    pallas_call x1, Pallas kernels, body(): pl.pallas_call(finish, out_shape=(result,) * 4, in_specs=[vmem] * 4, out_...  1 us

profile of v3, /device:TPU:1, one launch (start us, length us, event | category | flops | bytes accessed | tf_op | source)
XLA Modules:
  0.0 42.1 jit_solution(6231555652095701936)
XLA Ops:
  0.6 40.5 %attention.1 = (f32[128,512]{1,0:T(8,128)S(1)}, f32[128,512]{1,0:T(8,128)S(1)}, f32[128,512]{1,0:T(8,128)S(1)}, f32[128,512]{1,0:T(8,128)S(1)}) custom-call(s32[4]{0:T(128)} %exps_in.1, s32[1,128]{1,0:T(1,128)} %bitcast.3, bf16[128,512]{1,0:T(8,128)(2,1)} %q_in.1, bf16[128,512]{1,0:T(8,128)(2,1)} %k_in.1, bf16[128,512]{1,0:T(8,128)(2,1)} %v_in.1, ...), custom_call_target="tpu_custom_call" | custom-call | tf_op jit(solution)/shard_map/attention/pallas_call | solution.py:535
  41.1 1.0 %finish.1 = (f32[128,512]{1,0:T(8,128)}, f32[128,512]{1,0:T(8,128)}, f32[128,512]{1,0:T(8,128)}, f32[128,512]{1,0:T(8,128)}) custom-call(f32[128,512]{1,0:T(8,128)S(1)} %get-tuple-element.8.refs_0_, f32[128,512]{1,0:T(8,128)S(1)} %get-tuple-element.9.refs_1_, f32[128,512]{1,0:T(8,128)S(1)} %get-tuple-element.10.refs_2_, f32[128,512]{1,0:T(8,128)S(1)} %get-tuple-element.11.refs_3_), custom_call_target="tpu_custom_call" | custom-call | tf_op jit(solution)/shard_map/finish/pallas_call | solution.py:584

commit v4 on v3

--- a/solution.py
+++ b/solution.py
@@ -216,6 +216,24 @@
     rmeta[y] = chip_meta
     same_chip = [(lasts[0] == lasts[1]).astype(F32), (firsts[0] == firsts[1]).astype(F32)]
 
+    def row_send(way, i, n, j):
+        rows = pl.ds(pl.multiple_of(j * width, width), width)
+        return copy(
+            chip.at[way, i, rows], there.at[way, i, y], t_send.at[way, i, n], t_recv.at[way, i, y], at(z, j, c)
+        )
+
+    def meta_send(n, j):
+        return copy(cmeta, rmeta.at[y], m_send.at[1 + n], m_recv.at[1 + y], at(z, j, c))
+
+    def back_send(way, i, n, j):
+        rows = pl.ds(pl.multiple_of(y * width, width), width)
+        return copy(
+            slices.at[way, i, j], raw.at[way, i, rows], b_send.at[way, i, n], b_recv.at[way, i, y], at(z, j, c)
+        )
+
+    def core_send(way, i):
+        return copy(give.at[way, i], state.at[way, mine[i]], e_send.at[way, i], e_recv.at[way, i], partner)
+
     def to_row(way):
         for i in range(OWN):
             first_copies[way][i].wait_recv()
@@ -225,37 +243,37 @@
             whole = mine * local[way, OWN * c + i] + theirs * part[way, i]
             chip[way, i] = whole
             for n, j in enumerate(in_row):
-                sends.append(
-                    copy(
-                        chip.at[way, i, pl.ds(pl.multiple_of(j * width, width), width)],
-                        there.at[way, i, y],
-                        t_send.at[way, i, n],
-                        t_recv.at[way, i, y],
-                        at(z, j, c),
-                    )
-                )
-                sends[-1].start()
+                row_send(way, i, n, j).start()
             there[way, i, y] = chip[way, i, pl.ds(pl.multiple_of(y * width, width), width), :]
 
-    to_row(0)
-    for n, j in enumerate(in_row):
-        sends.append(copy(cmeta, rmeta.at[y], m_send.at[1 + n], m_recv.at[1 + y], at(z, j, c)))
-        sends[-1].start()
-
-    @pl.when(last_out)
-    def _():
-        wait_for(fetches[6:])
-        local_states(1, theirs, their_rates)
-        for first_copy in first_copies[1]:
-            first_copy.start()
-        local_states(1, mine, own_rates)
-
-
-    to_row(1)
-
-    @pl.when(last_out)
-    def _():
-        in_blocks()
+    def send_meta():
+        for n, j in enumerate(in_row):
+            meta_send(n, j).start()
+
+    @pl.when(z == 0)
+    def _():
+        to_row(0)
+        send_meta()
+
+        @pl.when(last_out)
+        def _():
+            wait_for(fetches[6:])
+            local_states(1, theirs, their_rates)
+            for first_copy in first_copies[1]:
+                first_copy.start()
+            local_states(1, mine, own_rates)
+
+        to_row(1)
+
+        @pl.when(last_out)
+        def _():
+            in_blocks()
+
+    @pl.when(z != 0)
+    def _():
+        to_row(1)
+        send_meta()
+        to_row(0)
 
     gifts = [
         copy(given, got.at[0], g_send.at[0], g_recv.at[0], partner),
@@ -318,11 +336,6 @@
                 z_copy(way, 2, i).start()
 
 
-    to_rows(0)
-    to_rows(1)
-
-    edge = [None, None]
-
     def to_chips(way):
         order = orders[way]
         for i in range(OWN):
@@ -334,7 +347,6 @@
 
             if i == 0:
                 near, far = zrecv[way, 0, 0:1], zrecv[way, 1, 0:1]
-                edge[way] = near
             span = jnp.exp(-own_rates[i] * (2 * BLK))
             row_span = jnp.exp(-own_rates[i] * (2 * BLK * ROW)) * (near == far).astype(F32)
             rows = slice(8 + i * width, 8 + (i + 1) * width)
@@ -350,27 +362,28 @@
                 here = end_of(way, j)
                 keep = keep * span * (here == there_end).astype(F32)
                 there_end = here
+            for n, j in enumerate(in_row):
+                back_send(way, i, n, j).start()
             here = pl.ds(pl.multiple_of(y * width, width), width)
-            for n, j in enumerate(in_row):
-                sends.append(
-                    copy(
-                        slices.at[way, i, j],
-                        raw.at[way, i, here],
-                        b_send.at[way, i, n],
-                        b_recv.at[way, i, y],
-                        at(z, j, c),
-                    )
-                )
-                sends[-1].start()
             raw[way, i, here] = slices[way, i, y]
 
-    to_chips(0)
-    to_chips(1)
+    @pl.when(z == 0)
+    def _():
+        for way in (0, 1):
+            to_rows(way)
+            to_chips(way)
+
+    @pl.when(z != 0)
+    def _():
+        to_rows(1)
+        to_rows(0)
+        to_chips(0)
+        to_chips(1)
 
     beside = []
     for way in (0, 1):
         neighbour = rmeta[(y + ROW - 1) % ROW, 1:2, :] if way == 0 else rmeta[(y + 1) % ROW, 0:1, :]
-        beside.append(jnp.where(y == (0 if way == 0 else ROW - 1), edge[way], neighbour))
+        beside.append(jnp.where(y == (0 if way == 0 else ROW - 1), zrecv[way, 0, 0:1], neighbour))
 
     def to_core(way):
         inner = lasts[0] if way == 0 else firsts[1]
@@ -385,16 +398,7 @@
             between = jnp.where(c == way, local[way, OWN * c + i], part[way, i])
             inside = between + jnp.exp(-own_rates[i] * BLK) * kept * outer
             give[way, i] = jnp.where(c == way, inside, outer)
-            sends.append(
-                copy(
-                    give.at[way, i],
-                    state.at[way, OWN * c + i],
-                    e_send.at[way, i],
-                    e_recv.at[way, i],
-                    partner,
-                )
-            )
-            sends[-1].start()
+            core_send(way, i).start()
             state[way, OWN * c + i] = jnp.where(c == way, outer, inside)
 
     def from_core(way):
@@ -484,6 +488,14 @@
                 end_wait(way, i)
 
     out_copy.wait_recv()
+    for n, j in enumerate(in_row):
+        meta_send(n, j).wait_send()
+    for way in (0, 1):
+        for i in range(OWN):
+            for n, j in enumerate(in_row):
+                row_send(way, i, n, j).wait_send()
+                back_send(way, i, n, j).wait_send()
+            core_send(way, i).wait_send()
     for sent in sends:
         sent.wait_send()
     for w, n in hops:

time: 42.3 us -> 40.3 us (0.953)
  Pallas kernels: 41.5 us -> 39.5 us
    pallas_call x1, Pallas kernels: 40.5 us -> 38.5 us  [body(): pl.pallas_call(functools.partial(kernel, zs, xs), out_shape=(result,) * 4...]
where the time goes in v4:
time: 40.3 us; the launch traced here: 40.2 us
  Pallas kernels  39.5 us (98%)
  between operations  0.64 us (2%)
    pallas_call x1, Pallas kernels, body(): pl.pallas_call(functools.partial(kernel, zs, xs), out_shape=(result,) * 4...  38.5 us
    pallas_call x1, Pallas kernels, body(): pl.pallas_call(finish, out_shape=(result,) * 4, in_specs=[vmem] * 4, out_...  1 us

profile of v4, /device:TPU:1, one launch (start us, length us, event | category | flops | bytes accessed | tf_op | source)
XLA Modules:
  0.0 40.2 jit_solution(3520613040577891632)
XLA Ops:
  0.6 38.5 %attention.1 = (f32[128,512]{1,0:T(8,128)S(1)}, f32[128,512]{1,0:T(8,128)S(1)}, f32[128,512]{1,0:T(8,128)S(1)}, f32[128,512]{1,0:T(8,128)S(1)}) custom-call(s32[4]{0:T(128)} %exps_in.1, s32[1,128]{1,0:T(1,128)} %bitcast.3, bf16[128,512]{1,0:T(8,128)(2,1)} %q_in.1, bf16[128,512]{1,0:T(8,128)(2,1)} %k_in.1, bf16[128,512]{1,0:T(8,128)(2,1)} %v_in.1, ...), custom_call_target="tpu_custom_call" | custom-call | tf_op jit(solution)/shard_map/attention/pallas_call | solution.py:547
  39.2 1.0 %finish.1 = (f32[128,512]{1,0:T(8,128)}, f32[128,512]{1,0:T(8,128)}, f32[128,512]{1,0:T(8,128)}, f32[128,512]{1,0:T(8,128)}) custom-call(f32[128,512]{1,0:T(8,128)S(1)} %get-tuple-element.8.refs_0_, f32[128,512]{1,0:T(8,128)S(1)} %get-tuple-element.9.refs_1_, f32[128,512]{1,0:T(8,128)S(1)} %get-tuple-element.10.refs_2_, f32[128,512]{1,0:T(8,128)S(1)} %get-tuple-element.11.refs_3_), custom_call_target="tpu_custom_call" | custom-call | tf_op jit(solution)/shard_map/finish/pallas_call | solution.py:596

commit v5 on v4

--- a/solution.py
+++ b/solution.py
@@ -79,10 +79,8 @@
     for fetch in fetches:
         fetch.start()
     barrier = pltpu.get_barrier_semaphore()
-    others = [at(z, j, c) for j in in_row] + [(s, (x + n) % xs) for n in x_first]
-    others += [(partner[0], (x + n) % xs) for n in x_first] + [partner]
-    for device in others:
-        pl.semaphore_signal(barrier, inc=1, device_id=device, device_id_type=MESH)
+    others = [partner] + [at(z, j, c) for j in in_row]
+    others += [(at_s, (x + n) % xs) for n in x_first for at_s in (s, partner[0])]
     hops = [(w, n) for w in (0, 1) for n in (1, 2)]
     for w, n in hops:
 
@@ -90,6 +88,8 @@
         def _():
             pl.semaphore_signal(barrier, inc=1, device_id=hop(w, n), device_id_type=MESH)
 
+    for device in others:
+        pl.semaphore_signal(barrier, inc=1, device_id=device, device_id_type=MESH)
     for w, n in hops:
 
         @pl.when(before(w) < n)
@@ -422,6 +422,20 @@
         outw[1, i] = jnp.exp(-their_rates[i] * (BLK - place)) * leaves
     for gift in gifts:
         gift.wait_recv()
+    for n, j in enumerate(in_row):
+        meta_send(n, j).wait_send()
+    for way in (0, 1):
+        for i in range(OWN):
+            for n, j in enumerate(in_row):
+                row_send(way, i, n, j).wait_send()
+    for sent in sends:
+        sent.wait_send()
+    for w, n in hops:
+        for i in range(OWN):
+
+            @pl.when(after(w) >= n)
+            def _():
+                z_copy(w, n, i).wait_send()
 
     to_core(0)
 
@@ -454,7 +468,6 @@
         sent.start()
     out_copy = copy(pout, outgot, o_send.at[0], o_recv.at[0], partner)
     out_copy.start()
-    sends.append(out_copy)
     xrecv[c, x] = xsend[0]
 
     to_core(1)
@@ -488,23 +501,12 @@
                 end_wait(way, i)
 
     out_copy.wait_recv()
-    for n, j in enumerate(in_row):
-        meta_send(n, j).wait_send()
     for way in (0, 1):
         for i in range(OWN):
             for n, j in enumerate(in_row):
-                row_send(way, i, n, j).wait_send()
                 back_send(way, i, n, j).wait_send()
             core_send(way, i).wait_send()
-    for sent in sends:
-        sent.wait_send()
-    for w, n in hops:
-        for i in range(OWN):
-
-            @pl.when(after(w) >= n)
-            def _():
-                z_copy(w, n, i).wait_send()
-
+    out_copy.wait_send()
     for m in (c, 1 - c):
         for n in (x_first if m is c else [*x_first, 0]):
             from_x = (x + n) % xs

time: 40.3 us -> 40.3 us (level)
  no operation moved by 1% of the time
where the time goes in v5:
time: 40.3 us; the launch traced here: 40.2 us
  Pallas kernels  39.5 us (98%)
  between operations  0.64 us (2%)
    pallas_call x1, Pallas kernels, body(): pl.pallas_call(functools.partial(kernel, zs, xs), out_shape=(result,) * 4...  38.5 us
    pallas_call x1, Pallas kernels, body(): pl.pallas_call(finish, out_shape=(result,) * 4, in_specs=[vmem] * 4, out_...  1 us

profile of v5, /device:TPU:1, one launch (start us, length us, event | category | flops | bytes accessed | tf_op | source)
XLA Modules:
  0.0 40.2 jit_solution(304559459877703534)
XLA Ops:
  0.6 38.5 %attention.1 = (f32[128,512]{1,0:T(8,128)S(1)}, f32[128,512]{1,0:T(8,128)S(1)}, f32[128,512]{1,0:T(8,128)S(1)}, f32[128,512]{1,0:T(8,128)S(1)}) custom-call(s32[4]{0:T(128)} %exps_in.1, s32[1,128]{1,0:T(1,128)} %bitcast.3, bf16[128,512]{1,0:T(8,128)(2,1)} %q_in.1, bf16[128,512]{1,0:T(8,128)(2,1)} %k_in.1, bf16[128,512]{1,0:T(8,128)(2,1)} %v_in.1, ...), custom_call_target="tpu_custom_call" | custom-call | tf_op jit(solution)/shard_map/attention/pallas_call | solution.py:549
  39.2 1.0 %finish.1 = (f32[128,512]{1,0:T(8,128)}, f32[128,512]{1,0:T(8,128)}, f32[128,512]{1,0:T(8,128)}, f32[128,512]{1,0:T(8,128)}) custom-call(f32[128,512]{1,0:T(8,128)S(1)} %get-tuple-element.8.refs_0_, f32[128,512]{1,0:T(8,128)S(1)} %get-tuple-element.9.refs_1_, f32[128,512]{1,0:T(8,128)S(1)} %get-tuple-element.10.refs_2_, f32[128,512]{1,0:T(8,128)S(1)} %get-tuple-element.11.refs_3_), custom_call_target="tpu_custom_call" | custom-call | tf_op jit(solution)/shard_map/finish/pallas_call | solution.py:598
